TPU v7x, 32 devices: a whole 2x2x4 slice. The times are simulated.
32 devices in a mesh: dp: 8 (over z, x), rep: 4 (over y, core).
Axes of the slice: x: 2, y: 2, z: 4, core: 2. Of those that a mesh axis runs over, the one named last changes fastest.
Arguments:
- patches: bfloat16 [512, 50, 1024], P(('dp', 'rep')), may hold values from -6 to 6
- keep: int32 [512, 50], P(('dp', 'rep')), may hold values from 0 to 1, as said below
- ln1_gain: float32 [1024], replicated, may hold values from 0.5 to 1.5
- ln1_bias: float32 [1024], replicated, may hold values from -3 to 3
- w_qkv: bfloat16 [1024, 3072], replicated, may hold values from -0.1875 to 0.1875
- b_query: float32 [1024], replicated, may hold values from -3 to 3
- b_value: float32 [1024], replicated, may hold values from -3 to 3
- w_out: bfloat16 [1024, 1024], replicated, may hold values from -0.4375 to 0.4375
- b_out: float32 [1024], replicated, may hold values from -3 to 3
- ln2_gain: float32 [1024], replicated, may hold values from 0.5 to 1.5
- ln2_bias: float32 [1024], replicated, may hold values from -3 to 3
- w_fc1: bfloat16 [1024, 4096], replicated, may hold values from -0.1875 to 0.1875
- b_fc1: float32 [4096], replicated, may hold values from -3 to 3
- w_fc2: bfloat16 [4096, 1024], replicated, may hold values from -0.125 to 0.125
- b_fc2: float32 [1024], replicated, may hold values from -3 to 3
- cotangent: bfloat16 [512, 50, 1024], P(('dp', 'rep')), may hold values from -6 to 6
Outputs:
- layer_out: bfloat16 [512, 50, 1024], P(('dp', 'rep'))
- grad_patches: float32 [512, 50, 1024], P(('dp', 'rep'))
- grad_ln1_gain: float32 [1024], P(('dp', 'rep'))
- grad_ln1_bias: float32 [1024], P(('dp', 'rep'))
- grad_w_qkv: float32 [1024, 3072], P(('dp', 'rep'))
- grad_b_query: float32 [1024], P(('dp', 'rep'))
- grad_b_value: float32 [1024], P(('dp', 'rep'))
- grad_w_out: float32 [1024, 1024], P(('dp', 'rep'))
- grad_b_out: float32 [1024], P(('dp', 'rep'))
- grad_ln2_gain: float32 [1024], P(('dp', 'rep'))
- grad_ln2_bias: float32 [1024], P(('dp', 'rep'))
- grad_w_fc1: float32 [1024, 4096], P(('dp', 'rep'))
- grad_b_fc1: float32 [4096], P(('dp', 'rep'))
- grad_w_fc2: float32 [4096, 1024], P(('dp', 'rep'))
- grad_b_fc2: float32 [1024], P(('dp', 'rep'))
Inputs may be any that keep to these rules, and one draw needn't show every extreme that they name: `keep`: each row keeps position 0 and between 25 and 50 positions in all; some image keeps exactly 50 and some exactly 25.
All inputs are finite; a program needn't handle non-finite values.
Results may differ from a plain program's by a relative error of at most 0.011.
Values sent between devices are 32-bit elements; how exact they have to be, the bound alone decides.
A program may use at most 256 MiB of HBM per device.

v0:
```python
from functools import partial

import jax
import jax.numpy as jnp
from jax import lax
from jax.sharding import PartitionSpec as P

HEADS = 16
HEAD_DIM = 64


NORM_EPSILON = 1e-06
SCORE_SCALE = 0.125


def select_parts(keep, slot_count):
    slot_ids = jnp.arange(slot_count, dtype=jnp.int32)
    ranks = jnp.cumsum(keep, axis=1) - 1
    table = (ranks[:, None, :] == slot_ids[None, :, None]) & (keep[:, None, :] == 1)
    counts = jnp.sum(keep, axis=1)
    valid_slots = (slot_ids[None, :] < counts[:, None]).astype(jnp.float32)
    return (table.astype(jnp.float32), valid_slots)


def normalize(v):
    centred = v - jnp.mean(v, axis=-1, keepdims=True)
    return centred * lax.rsqrt(jnp.mean(centred * centred, axis=-1, keepdims=True) + NORM_EPSILON)


def affine_norm(v, gain, shift):
    return normalize(v) * gain + shift


def matmul(left, right):
    return jnp.dot(left, right, preferred_element_type=jnp.float32)


def local(
    patches,
    keep,
    ln1_gain,
    ln1_bias,
    w_qkv,
    b_query,
    b_value,
    w_out,
    b_out,
    ln2_gain,
    ln2_bias,
    w_fc1,
    b_fc1,
    w_fc2,
    b_fc2,
    cotangent,
):
    images, slot_count, width = patches.shape
    row_count = images * slot_count
    table, valid_slots = select_parts(keep, slot_count)
    kept = jnp.einsum(
        "bsp,bpd->bsd", table.astype(jnp.bfloat16), patches, preferred_element_type=jnp.float32
    ).reshape(row_count, width)
    normed_one, norm_one_back = jax.vjp(affine_norm, kept, ln1_gain, ln1_bias)
    act_one = normed_one.astype(jnp.bfloat16)
    bias_all = jnp.concatenate([b_query, jnp.zeros_like(b_query), b_value])
    qkv = (matmul(act_one, w_qkv) + bias_all).astype(jnp.bfloat16)
    qkv = qkv.reshape(images, slot_count, 3, HEADS, HEAD_DIM)
    queries, key_part, values = (qkv[:, :, 0], qkv[:, :, 1], qkv[:, :, 2])
    scores = (
        jnp.einsum("blhe,bmhe->bhlm", queries, key_part, preferred_element_type=jnp.float32)
        * SCORE_SCALE
    )
    scores = jnp.where(valid_slots[:, None, None, :] > 0, scores, -1000000000.0)
    attn_probs, softmax_back = jax.vjp(partial(jax.nn.softmax, axis=-1), scores)
    probs_low = attn_probs.astype(jnp.bfloat16)
    mixed_heads = jnp.einsum(
        "bhlm,bmhe->blhe", probs_low, values, preferred_element_type=jnp.float32
    )
    mixed_heads = mixed_heads.reshape(row_count, width).astype(jnp.bfloat16)
    after_attn = kept + (matmul(mixed_heads, w_out) + b_out)
    normed_two, norm_two_back = jax.vjp(affine_norm, after_attn, ln2_gain, ln2_bias)
    act_two = normed_two.astype(jnp.bfloat16)
    pre_gelu = matmul(act_two, w_fc1) + b_fc1
    gelu_full, gelu_back = jax.vjp(partial(jax.nn.gelu, approximate=False), pre_gelu)
    gelu_out = gelu_full.astype(jnp.bfloat16)
    mlp_out = matmul(gelu_out, w_fc2) + b_fc2
    row_mask = valid_slots.reshape(row_count, 1)
    layer_out = ((after_attn + mlp_out) * row_mask).astype(jnp.bfloat16)
    layer_out = layer_out.reshape(images, slot_count, width)
    grad_out = cotangent.astype(jnp.float32).reshape(row_count, width) * row_mask
    grad_top = grad_out.astype(jnp.bfloat16)
    grad_w_fc2 = matmul(gelu_out.T, grad_top)
    grad_b_fc2 = jnp.sum(grad_top.astype(jnp.float32), axis=0)
    (grad_pre_full,) = gelu_back(matmul(grad_top, w_fc2.T))
    grad_pre = grad_pre_full.astype(jnp.bfloat16)
    grad_w_fc1 = matmul(act_two.T, grad_pre)
    grad_b_fc1 = jnp.sum(grad_pre.astype(jnp.float32), axis=0)
    grad_norm_two, grad_ln2_gain, grad_ln2_bias = norm_two_back(matmul(grad_pre, w_fc1.T))
    grad_after = grad_out + grad_norm_two
    mlp_grads = (grad_w_fc1, grad_b_fc1, grad_w_fc2, grad_b_fc2, grad_ln2_gain, grad_ln2_bias)
    mlp_half = (
        lax.psum_scatter(mlp_grads[0], "dp", scatter_dimension=0, tiled=True),
        lax.psum_scatter(mlp_grads[1], "dp", scatter_dimension=0, tiled=True),
        lax.psum_scatter(mlp_grads[2], "dp", scatter_dimension=0, tiled=True),
        lax.psum_scatter(mlp_grads[3], "dp", scatter_dimension=0, tiled=True),
        lax.psum_scatter(mlp_grads[4], "dp", scatter_dimension=0, tiled=True),
        lax.psum_scatter(mlp_grads[5], "dp", scatter_dimension=0, tiled=True),
    )
    mlp_shares = (
        lax.psum_scatter(mlp_half[0], "rep", scatter_dimension=0, tiled=True),
        lax.psum_scatter(mlp_half[1], "rep", scatter_dimension=0, tiled=True),
        lax.psum_scatter(mlp_half[2], "rep", scatter_dimension=0, tiled=True),
        lax.psum_scatter(mlp_half[3], "rep", scatter_dimension=0, tiled=True),
        lax.psum_scatter(mlp_half[4], "rep", scatter_dimension=0, tiled=True),
        lax.psum_scatter(mlp_half[5], "rep", scatter_dimension=0, tiled=True),
    )
    grad_branch = grad_after.astype(jnp.bfloat16)
    grad_w_out = matmul(mixed_heads.T, grad_branch)
    grad_b_out = jnp.sum(grad_branch.astype(jnp.float32), axis=0)
    grad_mixed = matmul(grad_branch, w_out.T).astype(jnp.bfloat16)
    grad_mixed = grad_mixed.reshape(images, slot_count, HEADS, HEAD_DIM)
    grad_probs = jnp.einsum(
        "blhe,bmhe->bhlm", grad_mixed, values, preferred_element_type=jnp.float32
    )
    grad_values = jnp.einsum(
        "bhlm,blhe->bmhe", probs_low, grad_mixed, preferred_element_type=jnp.float32
    )
    (grad_scores_full,) = softmax_back(grad_probs)
    grad_scores = grad_scores_full.astype(jnp.bfloat16)
    grad_queries = (
        jnp.einsum("bhlm,bmhe->blhe", grad_scores, key_part, preferred_element_type=jnp.float32)
        * SCORE_SCALE
    )
    grad_keys = (
        jnp.einsum("bhlm,blhe->bmhe", grad_scores, queries, preferred_element_type=jnp.float32)
        * SCORE_SCALE
    )
    grad_qkv = jnp.stack([grad_queries, grad_keys, grad_values], axis=2)
    grad_qkv = grad_qkv.reshape(row_count, 3 * width).astype(jnp.bfloat16)
    grad_w_qkv = matmul(act_one.T, grad_qkv)
    column_sums = jnp.sum(grad_qkv.astype(jnp.float32), axis=0)
    grad_b_query = column_sums[:width]
    grad_b_value = column_sums[2 * width :]
    grad_norm_one, grad_ln1_gain, grad_ln1_bias = norm_one_back(matmul(grad_qkv, w_qkv.T))
    grad_kept = grad_after + grad_norm_one
    attn_grads = (
        grad_w_qkv,
        grad_b_query,
        grad_b_value,
        grad_w_out,
        grad_b_out,
        grad_ln1_gain,
        grad_ln1_bias,
    )
    attn_half = (
        lax.psum_scatter(attn_grads[0], "dp", scatter_dimension=0, tiled=True),
        lax.psum_scatter(attn_grads[1], "dp", scatter_dimension=0, tiled=True),
        lax.psum_scatter(attn_grads[2], "dp", scatter_dimension=0, tiled=True),
        lax.psum_scatter(attn_grads[3], "dp", scatter_dimension=0, tiled=True),
        lax.psum_scatter(attn_grads[4], "dp", scatter_dimension=0, tiled=True),
        lax.psum_scatter(attn_grads[5], "dp", scatter_dimension=0, tiled=True),
        lax.psum_scatter(attn_grads[6], "dp", scatter_dimension=0, tiled=True),
    )
    attn_shares = (
        lax.psum_scatter(attn_half[0], "rep", scatter_dimension=0, tiled=True),
        lax.psum_scatter(attn_half[1], "rep", scatter_dimension=0, tiled=True),
        lax.psum_scatter(attn_half[2], "rep", scatter_dimension=0, tiled=True),
        lax.psum_scatter(attn_half[3], "rep", scatter_dimension=0, tiled=True),
        lax.psum_scatter(attn_half[4], "rep", scatter_dimension=0, tiled=True),
        lax.psum_scatter(attn_half[5], "rep", scatter_dimension=0, tiled=True),
        lax.psum_scatter(attn_half[6], "rep", scatter_dimension=0, tiled=True),
    )
    grad_patches = jnp.einsum(
        "bsp,bsd->bpd",
        table,
        grad_kept.reshape(images, slot_count, width),
        precision=lax.Precision.HIGHEST,
    )
    return (
        layer_out,
        grad_patches,
        attn_shares[5],
        attn_shares[6],
        attn_shares[0],
        attn_shares[1],
        attn_shares[2],
        attn_shares[3],
        attn_shares[4],
        mlp_shares[4],
        mlp_shares[5],
        mlp_shares[0],
        mlp_shares[1],
        mlp_shares[2],
        mlp_shares[3],
    )


def solution(mesh):
    in_specs = (
        P(("dp", "rep"), None, None),
        P(("dp", "rep"), None),
        P(),
        P(),
        P(),
        P(),
        P(),
        P(),
        P(),
        P(),
        P(),
        P(),
        P(),
        P(),
        P(),
        P(("dp", "rep"), None, None),
    )
    out_specs = (
        P(("dp", "rep"), None, None),
        P(("dp", "rep"), None, None),
        P(("dp", "rep")),
        P(("dp", "rep")),
        P(("dp", "rep"), None),
        P(("dp", "rep")),
        P(("dp", "rep")),
        P(("dp", "rep"), None),
        P(("dp", "rep")),
        P(("dp", "rep")),
        P(("dp", "rep")),
        P(("dp", "rep"), None),
        P(("dp", "rep")),
        P(("dp", "rep"), None),
        P(("dp", "rep")),
    )
    return jax.shard_map(local, mesh=mesh, in_specs=in_specs, out_specs=out_specs, check_vma=False)
```

profile of v0, /device:TPU:0, one launch (start us, length us, event | category | flops | bytes accessed | tf_op | source)
XLA Modules:
  0.0 1184.3 jit_solution(12209006712926793135)
XLA Ops:
  7.2 0.8 broadcast_compare_fusion.1
  8.1 0.8 reduce_sum.169
  8.9 0.9 reduce_window_sum.11
  9.8 6.0 fusion.52
  15.9 2.6 multiply_reduce_fusion.1
  18.4 3.4 reshape.232
  22.0 4.3 copy.66
  26.3 3.5 reshape.235
  29.8 0.6 fusion.42
  30.6 10.1 add_convert_fusion.1
  40.7 13.1 %reshape.233 = bf16[16,50,3,16,64]{4,3,2,1,0:T(8,128)(2,1)} reshape(bf16[800,3072]{1,0:T(8,128)(2,1)} %add_convert_fusion.1) | data formatting | bytes 9830400 | tf_op jit(solution)/shard_map/reshape | solution.py:66
  53.8 5.0 fusion.50
  58.9 5.5 fusion.14
  64.4 8.4 fusion.53
  72.8 4.3 convert_bitcast_fusion
  77.1 4.3 copy.65
  81.4 5.6 convert_element_type.112
  87.0 4.4 fusion.54
  91.9 40.5 %multiply_convert_fusion = (bf16[800,4096]{1,0:T(8,128)(2,1)}, f32[800,4096]{1,0:T(8,128)}, f32[800,4096]{1,0:T(8,128)}) fusion(f32[4096]{0:T(1024)S(1)} %copy-done.39, bf16[1024,4096]{1,0:T(8,128)(2,1)} %param.27, f32[800,1024]{1,0:T(8,128)S(1)} %get-tuple-element.108, f32[1024]{0:T(1024)S(1)} %copy-done.41, f32[1024]{0:T(1024)S(1)} %copy-done.34, ...), kind=kOutput, calls=%fused_computation.7 | convolution fusion | flops 6931251200 | bytes 44464384 | tf_op jit(solution)/shard_map/dot_general | solution.py:35
  132.5 22.4 %convert_reduce_fusion.1 = (f32[4096]{0:T(1024)}, bf16[800,4096]{1,0:T(8,128)(2,1)}) fusion(f32[800,4096]{1,0:T(8,128)} %get-tuple-element.93, bf16[4096,1024]{1,0:T(8,128)(2,1)} %param.29, f32[800,1024]{1,0:T(8,128)} %reshape.235, f32[800]{0:T(1024)S(1)} %reshape.238, f32[800,4096]{1,0:T(8,128)} %get-tuple-element.109, f32[4096]{0:T(1024)S(1)} %copy-done.39), kind=kOutput, calls=%fused_computation.5 | convolution fusion | flops 6768226304 | bytes 44469376 | tf_op jit(solution)/shard_map/dot_general | solution.py:35
  154.9 13.0 %multiply_reduce_fusion.2 = (f32[1024]{0:T(1024)S(1)}, f32[800]{0:T(1024)S(1)}, f32[1024]{0:T(1024)S(1)}, f32[800,1024]{1,0:T(8,128)S(1)}) fusion(f32[800,1024]{1,0:T(8,128)} %copy-done.8, f32[800]{0:T(1024)S(1)} %fusion.36, f32[800]{0:T(1024)S(1)} %broadcast_multiply_fusion.1, f32[1024]{0:T(1024)S(1)} %copy-done.34, ...), kind=kOutput, calls=%fused_computation.51 | convolution fusion | flops 6717436928 | bytes 21517696 | tf_op jit(solution)/shard_map/dot_general | solution.py:35
  167.9 1.0 fusion.48
  169.0 0.9 copy-done.12
  170.4 1.7 copy-done.10
  172.1 4.5 fusion.37
  176.7 0.6 copy-done.17
  177.3 3.9 add_convert_fusion.2
  181.2 2.6 convert_element_type.127
  183.8 5.0 convolution_convert_fusion
  188.8 5.9 reshape.236
  194.8 10.8 multiply_reduce_fusion
  205.5 7.9 multiply_convert_fusion.1
  213.5 3.8 multiply_bitcast_fusion
  217.3 3.9 multiply_bitcast_fusion.1
  221.2 6.1 fusion.19
  227.3 9.0 convert_reduce_fusion
  236.3 9.4 copy.70
  245.7 13.3 %convert_element_type.125 = bf16[800,3072]{1,0:T(8,128)(2,1)} reshape(bf16[16,50,3,16,64]{4,3,2,1,0:T(8,128)(2,1)} %copy.70) | data formatting | bytes 9830400 | tf_op jit(solution)/shard_map/convert_element_type | solution.py:138
  259.0 11.8 fusion.55
  270.9 15.8 %fusion.45 = f32[1024,4096]{1,0:T(8,128)} fusion(bf16[800,4096]{1,0:T(8,128)(2,1)} %get-tuple-element.115, f32[800,1024]{1,0:T(8,128)} %copy-done.8, f32[1024]{0:T(1024)S(1)} %copy-done.41, f32[1024]{0:T(1024)S(1)} %copy-done.34, f32[800]{0:T(1024)S(1)} %fusion.36, f32[800]{0:T(1024)S(1)} %broadcast_multiply_fusion.1), kind=kOutput, calls=%fused_computation.104 | convolution fusion | flops 6714982400 | bytes 26622208 | tf_op jit(solution)/shard_map/dot_general | solution.py:35
  286.8 16.2 %fusion.43 = f32[4096,1024]{1,0:T(8,128)} fusion(bf16[800,4096]{1,0:T(8,128)(2,1)} %get-tuple-element.92, f32[800,1024]{1,0:T(8,128)} %reshape.235, f32[800]{0:T(1024)S(1)} %reshape.238), kind=kOutput, calls=%fused_computation.102 | convolution fusion | flops 6712524800 | bytes 26610816 | tf_op jit(solution)/shard_map/dot_general | solution.py:35
  303.7 177.3 %reduce-scatter.9.cloned.1.call-done = f32[128,3072]{1,0:T(8,128)} async-done(((f32[1024,3072]{1,0:T(8,128)}), f32[128,3072]{1,0:T(8,128)}) %reduce-scatter.9.cloned.1.call-update) | async-done | bytes 1572880 | tf_op jit(solution)/shard_map/reduce_scatter | solution.py:155
  481.1 286.0 %reduce-scatter.17.cloned.1.call-done = f32[128,4096]{1,0:T(8,128)} async-done(((f32[1024,4096]{1,0:T(8,128)}), f32[128,4096]{1,0:T(8,128)}) %reduce-scatter.17.cloned.1.call-update) | async-done | bytes 2097168 | tf_op jit(solution)/shard_map/reduce_scatter | solution.py:101
  767.3 0.6 dynamic-slice.2
  769.2 0.6 dynamic-slice
  771.0 12.7 %multiply_convert_fusion.3 = bf16[800,1024]{1,0:T(8,128)(2,1)} fusion(f32[800,1024]{1,0:T(8,128)} %copy-done.8, f32[800]{0:T(1024)S(1)} %reshape.238, f32[1024]{0:T(1024)S(1)} %copy-done.42, bf16[800,4096]{1,0:T(8,128)(2,1)} %get-tuple-element.92, bf16[4096,1024]{1,0:T(8,128)(2,1)} %param.29), kind=kOutput, calls=%fused_computation.58 | convolution fusion | flops 6714163200 | bytes 19864704 | tf_op jit(solution)/shard_map/dot_general | solution.py:35
  783.7 2.6 reshape.234
  786.3 3.6 copy.72
  789.9 262.6 %reduce-scatter.21.cloned.1.call-done = f32[512,1024]{1,0:T(8,128)} async-done(((f32[4096,1024]{1,0:T(8,128)}), f32[512,1024]{1,0:T(8,128)}) %reduce-scatter.21.cloned.1.call-update) | async-done | bytes 2097168 | tf_op jit(solution)/shard_map/reduce_scatter | solution.py:103
  1052.7 1.8 convert_reduce_fusion.2
  1054.5 11.3 multiply_reduce_fusion.3
  1065.9 36.0 %all-reduce.18 = (f32[1024]{0:T(1024)S(1)}, f32[1024]{0:T(1024)S(1)}, f32[1024]{0:T(1024)S(1)}, f32[1024]{0:T(1024)S(1)}, f32[1024]{0:T(1024)S(1)}, /*index=5*/f...) all-reduce(f32[1024]{0:T(1024)S(1)} %get-tuple-element.62, ...), channel_id=2, replica_groups=mesh['dp'=8,'rep'=4] {'dp'}, use_global_device_ids=true, to_apply=%region_14.15.clone | all-reduce | flops 12288 | bytes 98304
  1102.6 5.7 all-reduce.19
  1108.3 0.6 dynamic-slice.3
  1108.9 0.6 dynamic-slice.7
  1111.8 0.6 dynamic-slice.27
  1113.0 4.0 fusion.47
  1117.2 2.1 add_add_fusion.2
  1119.3 3.6 reshape.237
  1122.8 3.7 fusion.29
  1126.5 3.6 copy.73
  1130.1 0.6 dynamic-slice.31
  1130.7 11.8 reduce-scatter.19.cloned.1.call-done
  1142.5 34.6 %reduce-scatter.23.cloned.1.call-done = f32[128,1024]{1,0:T(8,128)} async-done(((f32[512,1024]{1,0:T(8,128)}), f32[128,1024]{1,0:T(8,128)}) %reduce-scatter.23.cloned.1.call-update) | async-done | bytes 524304 | tf_op jit(solution)/shard_map/reduce_scatter | solution.py:111
  (148 shorter events, 6.6 us)
Async XLA Ops:
  7.2 79.8 %copy-start = (bf16[1024,1024]{1,0:T(8,128)(2,1)S(1)}, bf16[1024,1024]{1,0:T(8,128)(2,1)}, u32[]{:S(2)}) copy-start(bf16[1024,1024]{1,0:T(8,128)(2,1)} %param.23) | copy-start | bytes 6291460
  7.2 295.9 %reduce-scatter.13.cloned.1.call-start = ((), (), s32[]{:S(2)}) async-start(), calls=%async_computation.10 | async-start | bytes 4718592 | tf_op jit(solution)/shard_map/reduce_scatter | solution.py:158
  8.1 10.3 copy-start.25
  9.8 6.0 copy-start.18
  15.8 6.1 copy-start.16
  15.9 14.7 %copy-start.27 = (f32[800]{0:T(1024)}, f32[800]{0:T(1024)S(1)}, u32[]{:S(2)}) copy-start(f32[800]{0:T(1024)S(1)} %div.61) | copy-start | bytes 9604
  21.9 7.9 copy-start.20
  26.3 4.2 copy-start.35
  26.3 4.2 copy-start.36
  26.3 4.3 copy-start.32
  26.3 4.3 copy-start.37
  30.5 10.2 copy-start.22
  30.5 10.2 copy-start.29
  58.9 5.5 copy-start.1
  58.9 5.5 copy-start.3
  58.9 13.9 %copy-start.6 = (bf16[16,50,1,16,64]{4,3,2,1,0:T(8,128)(2,1)}, bf16[16,50,1,16,64]{4,3,2,1,0:T(8,128)(2,1)S(1)}, u32[]{:S(2)}) copy-start(bf16[16,50,1,16,64]{4,3,2,1,0:T(8,128)(2,1)S(1)} %get-tuple-element.96) | copy-start | bytes 4915204
  72.8 4.3 copy-start.5
  72.8 4.3 copy-start.14
  81.4 5.6 copy-start.40
  87.0 4.9 copy-start.34
  87.0 5.0 copy-start.39
  87.0 5.0 copy-start.41
  91.4 41.1 %copy-start.8 = (f32[800,1024]{1,0:T(8,128)}, f32[800,1024]{1,0:T(8,128)S(1)}, u32[]{:S(2)}) copy-start(f32[800,1024]{1,0:T(8,128)S(1)} %get-tuple-element.108) | copy-start | bytes 9830404
  154.9 13.0 %copy-start.9 = (f32[800,1024]{1,0:T(8,128)S(1)}, f32[800,1024]{1,0:T(8,128)}, u32[]{:S(2)}) copy-start(f32[800,1024]{1,0:T(8,128)} %copy-done.8) | copy-start | bytes 9830404
  167.9 1.9 copy-start.12
  169.9 2.3 copy-start.13
  170.4 1.7 copy-start.10
  176.6 0.7 copy-start.17
  176.6 0.7 copy-start.24
  176.6 0.7 copy-start.33
  176.6 0.7 copy-start.38
  176.6 304.4 %reduce-scatter.9.cloned.1.call-start = ((), (), s32[]{:S(2)}) async-start(), calls=%async_computation.8 | async-start | bytes 14155776 | tf_op jit(solution)/shard_map/reduce_scatter | solution.py:155
  188.8 5.9 copy-start.15
  205.5 7.9 copy-start.4
  213.5 3.8 copy-start.2
  213.5 7.7 slice-start
  217.3 3.9 slice-start.1
  221.2 6.1 copy-start.7
  270.9 496.2 %reduce-scatter.17.cloned.1.call-start = ((), (), s32[]{:S(2)}) async-start(), calls=%async_computation.12 | async-start | bytes 18874368 | tf_op jit(solution)/shard_map/reduce_scatter | solution.py:101
  286.7 765.8 %reduce-scatter.21.cloned.1.call-start = ((), (), s32[]{:S(2)}) async-start(), calls=%async_computation.14 | async-start | bytes 18874368 | tf_op jit(solution)/shard_map/reduce_scatter | solution.py:103
  303.0 464.1 %copy-start.21 = (f32[16,50]{1,0:T(8,128)S(1)}, f32[16,50]{1,0:T(8,128)}, u32[]{:S(2)}) copy-start(f32[16,50]{1,0:T(8,128)} %copy-done.20) | copy-start | bytes 9604
  303.0 464.2 %copy-start.44 = (u32[32]{0:T(128)S(1)}, u32[32]{0:T(128)}, u32[]{:S(2)}) copy-start(u32[32]{0:T(128)} %constant.107) | copy-start | bytes 388
  303.0 466.1 %copy-start.43 = (u32[32]{0:T(128)S(1)}, u32[32]{0:T(128)}, u32[]{:S(2)}) copy-start(u32[32]{0:T(128)} %constant.103) | copy-start | bytes 388
  303.1 468.0 %copy-start.42 = (f32[1024]{0:T(1024)S(1)}, f32[1024]{0:T(1024)}, u32[]{:S(2)}) copy-start(f32[1024]{0:T(1024)} %param.30) | copy-start | bytes 12292
  303.1 827.6 %reduce-scatter.15.cloned.1.call-start = ((), (), s32[]{:S(2)}) async-start(), calls=%async_computation.11 | async-start | bytes 655360 | tf_op jit(solution)/shard_map/reduce_scatter | solution.py:167
  303.7 827.0 %reduce-scatter.11.cloned.1.call-start = ((), (), s32[]{:S(2)}) async-start(), calls=%async_computation.9 | async-start | bytes 1966080 | tf_op jit(solution)/shard_map/reduce_scatter | solution.py:164
  481.0 661.4 %reduce-scatter.19.cloned.1.call-start = ((), (), s32[]{:S(2)}) async-start(), calls=%async_computation.13 | async-start | bytes 2621440 | tf_op jit(solution)/shard_map/reduce_scatter | solution.py:109
  767.1 409.9 %reduce-scatter.23.cloned.1.call-start = ((), (), s32[]{:S(2)}) async-start(), calls=%async_computation.15 | async-start | bytes 2621440 | tf_op jit(solution)/shard_map/reduce_scatter | solution.py:111
  786.3 268.2 %copy-start.28 = (f32[800]{0:T(1024)S(1)}, f32[800]{0:T(1024)}, u32[]{:S(2)}) copy-start(f32[800]{0:T(1024)} %copy-done.27) | copy-start | bytes 9604
  786.3 268.2 %copy-start.30 = (f32[800]{0:T(1024)S(1)}, f32[800]{0:T(1024)}, u32[]{:S(2)}) copy-start(f32[800]{0:T(1024)} %copy-done.29) | copy-start | bytes 9604
  1054.5 11.3 copy-start.31
  1054.5 58.4 %copy-start.23 = (f32[800]{0:T(1024)S(1)}, f32[800]{0:T(1024)}, u32[]{:S(2)}) copy-start(f32[800]{0:T(1024)} %copy-done.22) | copy-start | bytes 9604
  1113.0 4.2 copy-start.11
  1119.3 3.6 copy-start.19
  1119.3 3.6 copy-start.26
Sparse Core Ops, SparseCore 0:
  176.7 90.5 reduce-scatter.12
  271.3 209.6 reduce-scatter.8
  485.3 281.7 reduce-scatter.16
  770.7 281.7 reduce-scatter.20
  1055.6 20.7 reduce-scatter.14
  1079.3 28.1 reduce-scatter.10
  1110.8 31.6 reduce-scatter.18
  1145.6 31.4 reduce-scatter.22
where the time goes:
time: 1190 us; the launch traced here: 1180 us
  waiting for transfers between devices  773 us (65%)
  matrix products  212 us (18%)
  local copies, waits for them, and re-layouts  94.9 us (8%)
  other arithmetic  45.1 us (4%)
  blocking collectives  41.8 us (4%)
  between operations  17.8 us (1%)
    reduce_scatter x1, waiting for transfers between devices, local(): lax.psum_scatter(mlp_grads[0], 'dp', scatter_dimension=0, tiled=True)  286 us
    reduce_scatter x1, waiting for transfers between devices, local(): lax.psum_scatter(mlp_grads[2], 'dp', scatter_dimension=0, tiled=True)  263 us
    reduce_scatter x1, waiting for transfers between devices, local(): lax.psum_scatter(attn_grads[0], 'dp', scatter_dimension=0, tiled=True)  177 us
    dot_general x12, matrix products, matmul(): return jnp.dot(left, right, preferred_element_type=jnp.float32)  168 us
    unnamed x2, blocking collectives  41.8 us
    reduce_scatter x1, waiting for transfers between devices, local(): lax.psum_scatter(mlp_half[2], 'rep', scatter_dimension=0, tiled=True)  34.6 us
  transfers between devices with their start and end apart: 8, of which 5 were waited for; matrix products, arithmetic and copies ran while one was open for 15% of the time, Pallas kernels for 0%

commit v1 on v0

--- a/solution.py
+++ b/solution.py
@@ -33,6 +33,50 @@
 
 def matmul(left, right):
     return jnp.dot(left, right, preferred_element_type=jnp.float32)
+
+
+def exchange(parts, axis, stride, count):
+    size = lax.axis_size(axis)
+    index = lax.axis_index(axis)
+    place = (index // stride) % count
+    total = lax.dynamic_index_in_dim(parts, place, 0, keepdims=False)
+    for step in range(1, count):
+        pairs = []
+        for source in range(size):
+            own = (source // stride) % count
+            target = source + (((own + step) % count) - own) * stride
+            pairs.append((source, target))
+        sent = lax.dynamic_index_in_dim(parts, (place + step) % count, 0, keepdims=False)
+        total = total + lax.ppermute(sent, axis, pairs)
+    return total
+
+
+def scatter_sum(grad):
+    rows, columns = grad.shape
+    dp, rep = lax.axis_size("dp"), lax.axis_size("rep")
+    z, y = dp // 2, rep // 2
+    share = rows // (dp * rep)
+    parts = grad.reshape(z, 2, y, 2, share, columns)
+    parts = exchange(jnp.moveaxis(parts, 3, 0), "rep", 1, 2)
+    half = columns // 2
+    x_first, y_first = parts[..., :half], parts[..., half:]
+    x_first = exchange(jnp.moveaxis(x_first, 1, 0), "dp", 1, 2)
+    y_first = exchange(jnp.moveaxis(y_first, 2, 0), "rep", 2, y)
+    x_first = exchange(jnp.moveaxis(x_first, 1, 0), "rep", 2, y)
+    y_first = exchange(jnp.moveaxis(y_first, 1, 0), "dp", 1, 2)
+    both = jnp.concatenate([x_first, y_first], axis=-1)
+    return exchange(both, "dp", 2, z)
+
+
+def scatter_vectors(vectors):
+    joined = jnp.concatenate([v.reshape(lax.axis_size("dp") * lax.axis_size("rep"), -1) for v in vectors], axis=1)
+    total = lax.psum_scatter(joined, ("dp", "rep"), scatter_dimension=0, tiled=True)[0]
+    out, start = [], 0
+    for v in vectors:
+        length = v.shape[0] // (lax.axis_size("dp") * lax.axis_size("rep"))
+        out.append(total[start : start + length])
+        start += length
+    return out
 
 
 def local(
@@ -96,23 +140,8 @@
     grad_b_fc1 = jnp.sum(grad_pre.astype(jnp.float32), axis=0)
     grad_norm_two, grad_ln2_gain, grad_ln2_bias = norm_two_back(matmul(grad_pre, w_fc1.T))
     grad_after = grad_out + grad_norm_two
-    mlp_grads = (grad_w_fc1, grad_b_fc1, grad_w_fc2, grad_b_fc2, grad_ln2_gain, grad_ln2_bias)
-    mlp_half = (
-        lax.psum_scatter(mlp_grads[0], "dp", scatter_dimension=0, tiled=True),
-        lax.psum_scatter(mlp_grads[1], "dp", scatter_dimension=0, tiled=True),
-        lax.psum_scatter(mlp_grads[2], "dp", scatter_dimension=0, tiled=True),
-        lax.psum_scatter(mlp_grads[3], "dp", scatter_dimension=0, tiled=True),
-        lax.psum_scatter(mlp_grads[4], "dp", scatter_dimension=0, tiled=True),
-        lax.psum_scatter(mlp_grads[5], "dp", scatter_dimension=0, tiled=True),
-    )
-    mlp_shares = (
-        lax.psum_scatter(mlp_half[0], "rep", scatter_dimension=0, tiled=True),
-        lax.psum_scatter(mlp_half[1], "rep", scatter_dimension=0, tiled=True),
-        lax.psum_scatter(mlp_half[2], "rep", scatter_dimension=0, tiled=True),
-        lax.psum_scatter(mlp_half[3], "rep", scatter_dimension=0, tiled=True),
-        lax.psum_scatter(mlp_half[4], "rep", scatter_dimension=0, tiled=True),
-        lax.psum_scatter(mlp_half[5], "rep", scatter_dimension=0, tiled=True),
-    )
+    share_w_fc2 = scatter_sum(grad_w_fc2)
+    share_w_fc1 = scatter_sum(grad_w_fc1)
     grad_branch = grad_after.astype(jnp.bfloat16)
     grad_w_out = matmul(mixed_heads.T, grad_branch)
     grad_b_out = jnp.sum(grad_branch.astype(jnp.float32), axis=0)
@@ -142,32 +171,10 @@
     grad_b_value = column_sums[2 * width :]
     grad_norm_one, grad_ln1_gain, grad_ln1_bias = norm_one_back(matmul(grad_qkv, w_qkv.T))
     grad_kept = grad_after + grad_norm_one
-    attn_grads = (
-        grad_w_qkv,
-        grad_b_query,
-        grad_b_value,
-        grad_w_out,
-        grad_b_out,
-        grad_ln1_gain,
-        grad_ln1_bias,
-    )
-    attn_half = (
-        lax.psum_scatter(attn_grads[0], "dp", scatter_dimension=0, tiled=True),
-        lax.psum_scatter(attn_grads[1], "dp", scatter_dimension=0, tiled=True),
-        lax.psum_scatter(attn_grads[2], "dp", scatter_dimension=0, tiled=True),
-        lax.psum_scatter(attn_grads[3], "dp", scatter_dimension=0, tiled=True),
-        lax.psum_scatter(attn_grads[4], "dp", scatter_dimension=0, tiled=True),
-        lax.psum_scatter(attn_grads[5], "dp", scatter_dimension=0, tiled=True),
-        lax.psum_scatter(attn_grads[6], "dp", scatter_dimension=0, tiled=True),
-    )
-    attn_shares = (
-        lax.psum_scatter(attn_half[0], "rep", scatter_dimension=0, tiled=True),
-        lax.psum_scatter(attn_half[1], "rep", scatter_dimension=0, tiled=True),
-        lax.psum_scatter(attn_half[2], "rep", scatter_dimension=0, tiled=True),
-        lax.psum_scatter(attn_half[3], "rep", scatter_dimension=0, tiled=True),
-        lax.psum_scatter(attn_half[4], "rep", scatter_dimension=0, tiled=True),
-        lax.psum_scatter(attn_half[5], "rep", scatter_dimension=0, tiled=True),
-        lax.psum_scatter(attn_half[6], "rep", scatter_dimension=0, tiled=True),
+    share_w_out = scatter_sum(grad_w_out)
+    share_w_qkv = scatter_sum(grad_w_qkv)
+    small = scatter_vectors(
+        [grad_ln1_gain, grad_ln1_bias, grad_b_query, grad_b_value, grad_b_out, grad_ln2_gain, grad_ln2_bias, grad_b_fc1, grad_b_fc2]
     )
     grad_patches = jnp.einsum(
         "bsp,bsd->bpd",
@@ -178,19 +185,19 @@
     return (
         layer_out,
         grad_patches,
-        attn_shares[5],
-        attn_shares[6],
-        attn_shares[0],
-        attn_shares[1],
-        attn_shares[2],
-        attn_shares[3],
-        attn_shares[4],
-        mlp_shares[4],
-        mlp_shares[5],
-        mlp_shares[0],
-        mlp_shares[1],
-        mlp_shares[2],
-        mlp_shares[3],
+        small[0],
+        small[1],
+        share_w_qkv,
+        small[2],
+        small[3],
+        share_w_out,
+        small[4],
+        small[5],
+        small[6],
+        share_w_fc1,
+        small[7],
+        share_w_fc2,
+        small[8],
     )
 
 

time: 1190 us -> 780 us (0.66)
  waiting for transfers between devices: 773 us -> 149 us
  local copies, waits for them, and re-layouts: 94.9 us -> 180 us
  other arithmetic: 45.1 us -> 123 us
  starting transfers between devices: 0.32 us -> 54.5 us
  blocking collectives: 41.8 us -> 61.2 us
  between operations: 17.8 us -> 2.24 us
    reduce_scatter x8 -> x0, waiting for transfers between devices: 772 us -> none  [the longest x1 286 us: local(): lax.psum_scatter(mlp_grads[0], 'dp', scatter_dimension=0, tiled=True)]
    ppermute x0 -> x32, waiting for transfers between devices: none -> 149 us  [exchange(): total = total + lax.ppermute(sent, axis, pairs)]
    ppermute x0 -> x32, starting transfers between devices: none -> 54.5 us  [exchange(): total = total + lax.ppermute(sent, axis, pairs)]
    add x0 -> x25, other arithmetic: none -> 49.1 us  [the longest x24 49.1 us: exchange(): total = total + lax.ppermute(sent, axis, pairs)]
    convert_element_type x1, other arithmetic: 3.89 us -> 31.4 us  [local(): gelu_out = gelu_full.astype(jnp.bfloat16)]
    dot_general x0 -> x3, local copies, waits for them, and re-layouts: none -> 21.1 us  [matmul(): return jnp.dot(left, right, preferred_element_type=jnp.float32)]
    squeeze x0 -> x18, local copies, waits for them, and re-layouts: none -> 19.9 us  [exchange(): lax.dynamic_index_in_dim(parts, (place + step) % count, 0, keepdims=False)]
    unnamed x2 -> x1, blocking collectives: 41.8 us -> 61.2 us
  transfers between devices with their start and end apart: 8 -> 32, of which waited for: 5 -> 10; matrix products, arithmetic and copies ran while one was open for 15% -> 27% of each run, Pallas kernels for 0% -> 0%
where the time goes in v1:
time: 780 us; the launch traced here: 772 us
  matrix products  201 us (26%)
  local copies, waits for them, and re-layouts  180 us (23%)
  waiting for transfers between devices  149 us (19%)
  other arithmetic  123 us (16%)
  blocking collectives  61.2 us (8%)
  starting transfers between devices  54.5 us (7%)
    dot_general x12, matrix products, matmul(): return jnp.dot(left, right, preferred_element_type=jnp.float32)  163 us
    ppermute x32, waiting for transfers between devices, exchange(): total = total + lax.ppermute(sent, axis, pairs)  149 us
    unnamed x1, blocking collectives  61.2 us
    ppermute x32, starting transfers between devices, exchange(): total = total + lax.ppermute(sent, axis, pairs)  54.5 us
    add x24, other arithmetic, exchange(): total = total + lax.ppermute(sent, axis, pairs)  49.1 us
    convert_element_type x3, local copies, waits for them, and re-layouts, local(): grad_qkv = grad_qkv.reshape(row_count, 3 * width).astype(jnp.bfloat16)  36 us
    convert_element_type x1, other arithmetic, local(): gelu_out = gelu_full.astype(jnp.bfloat16)  31.4 us
    unnamed x132, local copies, waits for them, and re-layouts  22.4 us
  transfers between devices with their start and end apart: 32, of which 10 were waited for; matrix products, arithmetic and copies ran while one was open for 27% of the time, Pallas kernels for 0%

profile of v1, /device:TPU:0, one launch (start us, length us, event | category | flops | bytes accessed | tf_op | source)
XLA Modules:
  0.0 771.8 jit_solution(11792904358157352186)
XLA Ops:
  3.0 5.8 fusion.122
  8.9 3.5 reshape.350
  15.3 10.1 %add_convert_fusion.1 = bf16[800,3072]{1,0:T(8,128)(2,1)} fusion(bf16[1024,3072]{1,0:T(8,128)(2,1)} %param.20, f32[3072]{0:T(1024)S(1)} %pad_maximum_fusion, f32[800,1024]{1,0:T(8,128)} %reshape.350, f32[1024]{0:T(1024)S(1)} %copy-done.53, f32[1024]{0:T(1024)S(1)} %copy-done.55, f32[800]{0:T(1024)S(1)} %rsqrt.20, f32[800]{0:T(1024)S(1)} %div.98), kind=kOutput, calls=%fused_computation.44 | convolution fusion | flops 5042176000 | bytes 14510336 | tf_op jit(solution)/shard_map/dot_general | solution.py:35
  25.4 13.1 %reshape.351 = bf16[16,50,3,16,64]{4,3,2,1,0:T(8,128)(2,1)} reshape(bf16[800,3072]{1,0:T(8,128)(2,1)} %add_convert_fusion.1) | data formatting | bytes 9830400 | tf_op jit(solution)/shard_map/reshape | solution.py:110
  38.5 5.0 fusion.116
  43.6 5.5 fusion.38
  49.1 8.4 %fusion.123 = (f32[16,16,50]{2,1,0:T(8,128)S(1)}, f32[16,16,50,50]{2,3,1,0:T(8,128)S(1)}) fusion(f32[16,16,50,50]{2,3,1,0:T(8,128)} %fusion.38, pred[16,50]{1,0:T(8,128)(4,1)S(1)} %get-tuple-element.130), kind=kOutput, calls=%fused_computation.272 | output fusion | flops 3840049 | bytes 5172000 | tf_op jit(solution)/shard_map/jvp()/sub | solution.py:117
  58.3 4.0 convert_bitcast_fusion
  62.3 4.2 copy.104
  66.5 5.6 convert_element_type.113
  72.8 4.4 fusion.124
  79.9 2.9 copy.105
  82.8 3.7 reshape.353
  86.5 39.1 %fusion.1 = (f32[800,4096]{1,0:T(8,128)}, f32[800,4096]{1,0:T(8,128)}) fusion(f32[4096]{0:T(1024)S(1)} %copy-done.52, bf16[1024,4096]{1,0:T(8,128)(2,1)} %param.27, f32[800,1024]{1,0:T(8,128)} %copy-done.13, f32[1024]{0:T(1024)S(1)} %copy-done.63, f32[1024]{0:T(1024)S(1)} %copy-done.57, f32[800]{0:T(1024)S(1)} %fusion.105, f32[800]{0:T(1024)S(1)} %broadcast_multiply_fusion.1), kind=kOutput, calls=%fused_computation.5 | convolution fusion | flops 6921420800 | bytes 37910784 | tf_op jit(solution)/shard_map/dot_general | solution.py:35
  125.6 22.8 %convert_reduce_fusion.1 = (f32[4096]{0:T(1024)}, bf16[800,4096]{1,0:T(8,128)(2,1)}) fusion(f32[800,4096]{1,0:T(8,128)} %get-tuple-element.137, bf16[4096,1024]{1,0:T(8,128)(2,1)} %param.29, f32[800,1024]{1,0:T(8,128)} %reshape.353, f32[800]{0:T(1024)S(1)} %copy-done.50, f32[800,4096]{1,0:T(8,128)} %get-tuple-element.138, f32[4096]{0:T(1024)S(1)} %copy-done.52), kind=kOutput, calls=%fused_computation.26 | convolution fusion | flops 6768226304 | bytes 44469376 | tf_op jit(solution)/shard_map/dot_general | solution.py:35
  148.4 13.4 %multiply_reduce_fusion.2 = (f32[1024]{0:T(1024)}, f32[800]{0:T(1024)S(1)}, f32[1024]{0:T(1024)}, f32[800,1024]{1,0:T(8,128)S(1)}) fusion(f32[800,1024]{1,0:T(8,128)} %copy-done.13, f32[800]{0:T(1024)S(1)} %fusion.105, f32[800]{0:T(1024)S(1)} %broadcast_multiply_fusion.1, f32[1024]{0:T(1024)S(1)} %copy-done.57, bf16[800,4096]{1,0:T(8,128)(2,1)} %get-tuple-element.144, ...), kind=kOutput, calls=%fused_computation.102 | convolution fusion | flops 6717436928 | bytes 21517696 | tf_op jit(solution)/shard_map/dot_general | solution.py:35
  166.6 3.1 convolution_convert_fusion
  169.7 5.7 reshape.354
  175.3 8.2 %fusion.43 = bf16[16,50,1,16,64]{4,1,3,0,2:T(8,128)(2,1)} fusion(bf16[16,50,16,64]{3,2,1,0:T(8,128)(2,1)} %reshape.354, f32[16,16,50,50]{2,3,1,0:T(8,128)} %copy-done.6, f32[16,16,50]{2,1,0:T(8,128)S(1)} %copy-done.32), kind=kOutput, calls=%fused_computation.115 | convolution fusion | flops 83200000 | bytes 5888000 | tf_op jit(solution)/shard_map/bhlm,blhe->bmhe/dot_general | solution.py:153
  183.5 6.7 multiply_reduce_fusion
  190.3 7.4 multiply_convert_fusion.1
  201.9 12.1 %convert_reduce_fusion = (f32[3,16,64]{2,1,0:T(8,128)S(1)}, bf16[16,50,3,16,64]{4,1,3,0,2:T(8,128)(2,1)}) fusion(bf16[16,50,1,16,64]{4,1,3,0,2:T(8,128)(2,1)S(1)} %copy-done.30, bf16[16,50,1,16,64]{4,1,3,0,2:T(8,128)(2,1)S(1)} %multiply_bitcast_fusion, bf16[16,50,1,16,64]{4,1,3,0,2:T(8,128)(2,1)S(1)} %multiply_bitcast_fusion.1), kind=kLoop, calls=%fused_computation.2 | loop fusion | flops 9827328 | bytes 9842688 | tf_op jit(solution)/shard_map/reduce_sum | solution.py:169
  214.0 9.3 %copy.109 = bf16[16,50,3,16,64]{4,3,2,1,0:T(8,128)(2,1)} copy(bf16[16,50,3,16,64]{4,1,3,0,2:T(8,128)(2,1)} %get-tuple-element.86) | data formatting | bytes 9830400 | tf_op jit(solution)/shard_map/convert_element_type | solution.py:167
  223.3 13.3 %convert_element_type.126 = bf16[800,3072]{1,0:T(8,128)(2,1)} reshape(bf16[16,50,3,16,64]{4,3,2,1,0:T(8,128)(2,1)} %copy.109) | data formatting | bytes 9830400 | tf_op jit(solution)/shard_map/convert_element_type | solution.py:167
  236.6 13.4 %reshape.365 = bf16[800,3072,1,1,1,1]{1,0,2,3,4,5:T(8,128)(2,1)} reshape(bf16[16,50,3,16,64]{4,3,2,1,0:T(8,128)(2,1)} %copy.109) | data formatting | bytes 9830400 | tf_op jit(solution)/shard_map/convert_element_type | solution.py:167
  250.0 10.3 %multiply_reduce_fusion.3 = (f32[1024]{0:T(1024)S(1)}, f32[800]{0:T(1024)S(1)}, f32[1024]{0:T(1024)S(1)}, f32[800,1024]{1,0:T(8,128)S(1)}) fusion(f32[800,1024]{1,0:T(8,128)} %reshape.350, f32[800]{0:T(1024)S(1)} %copy-done.48, f32[800]{0:T(1024)S(1)} %copy-done.46, f32[1024]{0:T(1024)S(1)} %copy-done.56, bf16[800,3072]{1,0:T(8,128)(2,1)} %convert_element_type.126, ...), kind=kOutput, calls=%fused_computation.104 | convolution fusion | flops 5039715328 | bytes 17782144 | tf_op jit(solution)/shard_map/dot_general | solution.py:35
  260.4 3.0 fusion.114
  265.8 11.8 %fusion.30 = f32[4,2,2,2,32,3072]{5,4,3,2,1,0:T(8,128)} fusion(bf16[4,2,2,2,32,800]{5,4,3,2,1,0:T(8,128)(2,1)} %bitcast.294, bf16[800,3072,1,1,1,1]{1,0,2,3,4,5:T(8,128)(2,1)} %reshape.365), kind=kOutput, calls=%fused_computation.64 | convolution fusion | flops 5033164800 | bytes 19136512 | tf_op jit(solution)/shard_map/dot_general | solution.py:35
  277.6 6.3 dynamic-slice_bitcast_fusion.1
  284.4 2.9 copy.112
  287.3 4.8 fusion.49
  295.7 15.8 %fusion.111 = f32[1024,4096]{1,0:T(8,128)} fusion(bf16[800,4096]{1,0:T(8,128)(2,1)} %get-tuple-element.144, f32[800,1024]{1,0:T(8,128)} %copy-done.13, f32[1024]{0:T(1024)S(1)} %copy-done.63, f32[1024]{0:T(1024)S(1)} %copy-done.57, f32[800]{0:T(1024)S(1)} %fusion.105, f32[800]{0:T(1024)S(1)} %broadcast_multiply_fusion.1), kind=kOutput, calls=%fused_computation.260 | convolution fusion | flops 6714982400 | bytes 26622208 | tf_op jit(solution)/shard_map/dot_general | solution.py:35
  311.5 10.2 %constant_dynamic-slice_fusion.3 = (f32[4,2,2,1,32,4096]{5,4,3,2,1,0:T(8,128)}, f32[4,2,2,1,32,4096]{5,4,3,2,1,0:T(8,128)S(1)}) fusion(f32[4,2,2,2,32,4096]{5,4,3,2,1,0:T(8,128)} %bitcast.292, s32[]{:T(128)S(6)} %select_n.262, s32[]{:T(128)S(6)} %select_n.264), kind=kLoop, calls=%fused_computation.230 | loop fusion | bytes 33554440 | tf_op jit(solution)/shard_map/dynamic-slice.20
  321.7 3.9 copy.165
  326.2 31.4 %fusion.4 = bf16[4096,800]{0,1:T(8,128)(2,1)} fusion(f32[800,4096]{1,0:T(8,128)} %get-tuple-element.138, f32[4096]{0:T(1024)S(1)} %copy-done.52), kind=kLoop, calls=%fused_computation.8 | loop fusion | flops 216268800 | bytes 19677184 | tf_op jit(solution)/shard_map/convert_element_type | solution.py:128
  359.2 15.8 %dot_general.93 = bf16[4,2,2,2,128,800]{4,3,2,1,0,5:T(2,128)(2,1)} reshape(bf16[4096,800]{0,1:T(8,128)(2,1)} %fusion.4) | data formatting | bytes 13107200 | tf_op jit(solution)/shard_map/dot_general | solution.py:35
  378.7 12.0 %fusion.25 = f32[4,2,2,2,128,1024]{5,4,3,2,1,0:T(8,128)S(1)} fusion(bf16[4,2,2,2,128,800]{4,3,2,1,0,5:T(2,128)(2,1)} %dot_general.93, bf16[800,1024,1,1,1,1]{1,0,2,3,4,5:T(8,128)(2,1)} %reshape.367), kind=kOutput, calls=%fused_computation.57 | convolution fusion | flops 6710886400 | bytes 24969216 | tf_op jit(solution)/shard_map/dot_general | solution.py:35
  390.8 4.3 dynamic-slice_bitcast_fusion
  395.1 4.9 copy-done.7
  400.1 15.5 %multiply_convert_fusion.4 = bf16[800,1024]{1,0:T(8,128)(2,1)} fusion(f32[800,1024]{1,0:T(8,128)S(1)} %copy-done.15, f32[800]{0:T(1024)S(1)} %copy-done.50, f32[1024]{0:T(1024)S(1)} %copy-done.64, bf16[4096,1024]{1,0:T(8,128)(2,1)} %param.29, f32[800,4096]{1,0:T(8,128)} %get-tuple-element.137, f32[800,4096]{1,0:T(8,128)} %get-tuple-element.138, ...), kind=kOutput, calls=%fused_computation.109 | convolution fusion | flops 6727270400 | bytes 39541888 | tf_op jit(solution)/shard_map/dot_general | solution.py:35
  415.7 2.9 bitcast_add_fusion.7
  419.9 3.0 collective-permute-start.9
  427.4 3.5 reshape.355
  430.9 4.2 collective-permute-done.9
  439.8 4.2 collective-permute-done.10
  444.1 5.7 bitcast_add_fusion.2
  453.3 3.7 collective-permute-start.15
  460.0 3.3 fusion.76
  464.0 61.2 %all-reduce = f32[32,384]{1,0:T(8,128)S(1)} all-reduce(f32[32,384]{1,0:T(8,128)S(1)} %concatenate.19), channel_id=2, replica_groups=mesh['dp'=8,'rep'=4] {'dp','rep'}, use_global_device_ids=true, to_apply=%region_21.22.clone | all-reduce | flops 12288 | bytes 98304
  529.9 5.6 copy.120
  547.0 11.2 %bitcast_add_fusion.1 = f32[4,2,2,32,4096]{4,3,2,0,1:T(8,128)} fusion(f32[4,2,2,32,4096]{4,3,2,0,1:T(8,128)} %collective-permute-done.16, f32[4,2,2,1,32,4096]{5,4,3,2,1,0:T(8,128)} %get-tuple-element.91), kind=kLoop, calls=%fused_computation.46 | loop fusion | flops 2097152 | bytes 25165824 | tf_op jit(solution)/shard_map/add | solution.py:50
  558.3 4.0 fusion.118
  567.0 12.1 %bitcast_add_fusion = f32[4,2,2,128,1024]{4,3,2,1,0:T(8,128)} fusion(f32[4,2,2,128,1024]{4,3,2,1,0:T(8,128)} %collective-permute-done.24, f32[4,2,2,2,128,1024]{5,4,3,2,1,0:T(8,128)} %copy-done.7, s32[]{:T(128)S(6)} %select_n.262), kind=kLoop, calls=%fused_computation.45 | loop fusion | flops 2097152 | bytes 25165828 | tf_op jit(solution)/shard_map/add | solution.py:50
  582.1 3.9 collective-permute-start.7
  587.2 4.5 fusion.117
  592.1 3.4 collective-permute-done.7
  597.5 19.4 %collective-permute-done.6 = f32[32,3072]{1,0:T(8,128)S(1)} collective-permute-done((f32[32,3072]{1,0:T(8,128)S(1)}, f32[32,3072]{1,0:T(8,128)S(1)}, u32[]{:S(2)}, u32[]{:S(2)}) %collective-permute-start.6) | collective-permute-done | bytes 393248 | tf_op jit(solution)/shard_map/ppermute | solution.py:50
  625.3 32.2 %collective-permute-done.25 = f32[4,2,128,512]{3,2,1,0:T(8,128)S(1)} collective-permute-done((f32[4,2,128,512]{3,2,1,0:T(8,128)S(1)}, f32[4,2,128,512]{3,2,1,0:T(8,128)S(1)}, u32[]{:S(2)}, u32[]{:S(2)}) %collective-permute-start.25) | collective-permute-done | bytes 2097184 | tf_op jit(solution)/shard_map/ppermute | solution.py:50
  659.4 6.1 collective-permute-done.27
  667.6 20.4 %collective-permute-done.18 = f32[4,32,2048]{2,1,0:T(8,128)S(1)} collective-permute-done((f32[4,32,2048]{2,1,0:T(8,128)S(1)}, f32[4,32,2048]{2,1,0:T(8,128)S(1)}, u32[]{:S(2)}, u32[]{:S(2)}) %collective-permute-start.18) | collective-permute-done | bytes 1048608 | tf_op jit(solution)/shard_map/ppermute | solution.py:50
  690.4 15.7 %collective-permute-done.26 = f32[4,128,512]{2,1,0:T(8,128)S(1)} collective-permute-done((f32[4,128,512]{2,1,0:T(8,128)S(1)}, f32[4,128,512]{2,1,0:T(8,128)S(1)}, u32[]{:S(2)}, u32[]{:S(2)}) %collective-permute-start.26) | collective-permute-done | bytes 1048608 | tf_op jit(solution)/shard_map/ppermute | solution.py:50
  706.9 18.6 %collective-permute-start.29 = (f32[128,1024]{1,0:T(8,128)S(1)}, f32[128,1024]{1,0:T(8,128)S(1)}, u32[]{:S(2)}, u32[]{:S(2)}) collective-permute-start(f32[128,1024]{1,0:T(8,128)S(1)} %get-tuple-element.105), channel_id=1, source_target_pairs={{0,8},{4,12},{8,16},{12,20},{16,24},{20,28},{24,0},{28,4},{1,9},{5... | collective-permute-start | bytes 1572872 | tf_op jit(solution)/shard_map/ppermute | solution.py:50
  725.5 30.8 %collective-permute-done.22 = f32[32,4096]{1,0:T(8,128)S(1)} collective-permute-done((f32[32,4096]{1,0:T(8,128)S(1)}, f32[32,4096]{1,0:T(8,128)S(1)}, u32[]{:S(2)}, u32[]{:S(2)}) %collective-permute-start.22) | collective-permute-done | bytes 524320 | tf_op jit(solution)/shard_map/ppermute | solution.py:50
  757.2 13.1 %collective-permute-done.30 = f32[128,1024]{1,0:T(8,128)S(1)} collective-permute-done((f32[128,1024]{1,0:T(8,128)S(1)}, f32[128,1024]{1,0:T(8,128)S(1)}, u32[]{:S(2)}, u32[]{:S(2)}) %collective-permute-start.30) | collective-permute-done | bytes 524320 | tf_op jit(solution)/shard_map/ppermute | solution.py:50
  (270 shorter events, 93.4 us)
Async XLA Ops:
  0.6 72.1 %copy-start = (bf16[1024,1024]{1,0:T(8,128)(2,1)S(1)}, bf16[1024,1024]{1,0:T(8,128)(2,1)}, u32[]{:S(2)}) copy-start(bf16[1024,1024]{1,0:T(8,128)(2,1)} %param.23) | copy-start | bytes 6291460
  15.0 10.4 %copy-start.45 = (f32[800]{0:T(1024)}, f32[800]{0:T(1024)S(1)}, u32[]{:S(2)}) copy-start(f32[800]{0:T(1024)S(1)} %div.98) | copy-start | bytes 9604
  15.2 10.2 %copy-start.41 = (f32[800]{0:T(1024)}, f32[800]{0:T(1024)S(1)}, u32[]{:S(2)}) copy-start(f32[800]{0:T(1024)S(1)} %add.406) | copy-start | bytes 9604
  15.2 10.2 %copy-start.47 = (f32[800]{0:T(1024)}, f32[800]{0:T(1024)S(1)}, u32[]{:S(2)}) copy-start(f32[800]{0:T(1024)S(1)} %rsqrt.20) | copy-start | bytes 9604
  43.5 14.7 %copy-start.8 = (bf16[16,50,1,16,64]{4,3,2,1,0:T(8,128)(2,1)}, bf16[16,50,1,16,64]{4,3,2,1,0:T(8,128)(2,1)S(1)}, u32[]{:S(2)}) copy-start(bf16[16,50,1,16,64]{4,3,2,1,0:T(8,128)(2,1)S(1)} %get-tuple-element.95) | copy-start | bytes 4915204
  43.6 28.5 %copy-start.37 = (f32[16,50]{1,0:T(8,128)}, f32[16,50]{1,0:T(8,128)S(1)}, u32[]{:S(2)}) copy-start(f32[16,50]{1,0:T(8,128)S(1)} %get-tuple-element.129) | copy-start | bytes 9604
  86.5 39.1 %copy-start.50 = (f32[800]{0:T(1024)S(1)}, f32[800]{0:T(1024)}, u32[]{:S(2)}) copy-start(f32[800]{0:T(1024)} %reshape.364) | copy-start | bytes 9604
  148.4 13.4 %copy-start.40 = (f32[800]{0:T(1024)S(1)}, f32[800]{0:T(1024)}, u32[]{:S(2)}) copy-start(f32[800]{0:T(1024)} %copy-done.39) | copy-start | bytes 9604
  148.4 13.4 %copy-start.14 = (f32[800,1024]{1,0:T(8,128)S(1)}, f32[800,1024]{1,0:T(8,128)}, u32[]{:S(2)}) copy-start(f32[800,1024]{1,0:T(8,128)} %copy-done.13) | copy-start | bytes 9830404
  175.3 8.2 %copy-start.9 = (bf16[16,50,1,16,64]{4,3,2,1,0:T(8,128)(2,1)S(1)}, bf16[16,50,1,16,64]{4,3,2,1,0:T(8,128)(2,1)}, u32[]{:S(2)}) copy-start(bf16[16,50,1,16,64]{4,3,2,1,0:T(8,128)(2,1)} %copy-done.8) | copy-start | bytes 4915204
  175.3 8.2 %copy-start.10 = (bf16[16,50,16,64]{3,2,1,0:T(8,128)(2,1)S(1)}, bf16[16,50,16,64]{3,2,1,0:T(8,128)(2,1)}, u32[]{:S(2)}) copy-start(bf16[16,50,16,64]{3,2,1,0:T(8,128)(2,1)} %reshape.354) | copy-start | bytes 4915204
  175.3 8.2 %copy-start.33 = (f32[16,16,50]{2,1,0:T(8,128)S(1)}, f32[16,16,50]{2,1,0:T(8,128)}, u32[]{:S(2)}) copy-start(f32[16,16,50]{2,1,0:T(8,128)} %multiply_divide_fusion) | copy-start | bytes 153604
  190.3 7.4 copy-start.5
  236.6 13.4 %copy-start.46 = (f32[800]{0:T(1024)S(1)}, f32[800]{0:T(1024)}, u32[]{:S(2)}) copy-start(f32[800]{0:T(1024)} %copy-done.45) | copy-start | bytes 9604
  236.6 13.4 %copy-start.48 = (f32[800]{0:T(1024)S(1)}, f32[800]{0:T(1024)}, u32[]{:S(2)}) copy-start(f32[800]{0:T(1024)} %copy-done.47) | copy-start | bytes 9604
  236.6 13.4 %copy-start.56 = (f32[1024]{0:T(1024)S(1)}, f32[1024]{0:T(1024)}, u32[]{:S(2)}) copy-start(f32[1024]{0:T(1024)} %param.18) | copy-start | bytes 12292
  250.0 10.4 %copy-start.42 = (f32[800]{0:T(1024)S(1)}, f32[800]{0:T(1024)}, u32[]{:S(2)}) copy-start(f32[800]{0:T(1024)} %copy-done.41) | copy-start | bytes 9604
  250.0 10.4 %copy-start.16 = (f32[800,1024]{1,0:T(8,128)S(1)}, f32[800,1024]{1,0:T(8,128)}, u32[]{:S(2)}) copy-start(f32[800,1024]{1,0:T(8,128)} %reshape.350) | copy-start | bytes 9830404
  250.0 10.4 %copy-start.54 = (f32[1024]{0:T(1024)S(1)}, f32[1024]{0:T(1024)}, u32[]{:S(2)}) copy-start(f32[1024]{0:T(1024)} %param.19) | copy-start | bytes 12292
  284.0 160.1 %collective-permute-start = (f32[4,2,2,32,3072]{4,3,2,1,0:T(8,128)}, f32[4,2,2,32,3072]{4,3,2,1,0:T(8,128)}, u32[]{:S(2)}, u32[]{:S(2)}) collective-permute-start(f32[4,2,2,32,3072]{4,3,2,1,0:T(8,128)} %dynamic-slice_bitcast_fusion.1), channel_id=1, source_target_pairs={{0,1},{1,0},{2,3},{3,2},{4,5},{5,4},{6,7},{7,6},{8,9},{9,8},{10,11... | collective-permute-start | bytes 18874376 | tf_op jit(solution)/shard_map/ppermute | solution.py:50
  295.7 120.1 %collective-permute-start.8 = (f32[4,2,2,32,1024]{4,3,2,1,0:T(8,128)}, f32[4,2,2,32,1024]{4,3,2,1,0:T(8,128)}, u32[]{:S(2)}, u32[]{:S(2)}) collective-permute-start(f32[4,2,2,32,1024]{4,3,2,1,0:T(8,128)} %dynamic-slice_bitcast_fusion.5), channel_id=1, source_target_pairs={{0,1},{1,0},{2,3},{3,2},{4,5},{5,4},{6,7},{7,6},{8,9},{9,8},{10,11... | collective-permute-start | bytes 6291464 | tf_op jit(solution)/shard_map/ppermute | solution.py:50
  325.6 221.4 %collective-permute-start.16 = (f32[4,2,2,32,4096]{4,3,2,0,1:T(8,128)}, f32[4,2,2,32,4096]{4,3,2,0,1:T(8,128)}, u32[]{:S(2)}, u32[]{:S(2)}) collective-permute-start(f32[4,2,2,32,4096]{4,3,2,0,1:T(8,128)} %bitcast.290), channel_id=1, source_target_pairs={{0,1},{1,0},{2,3},{3,2},{4,5},{5,4},{6,7},{7,6},{8,9},{9,8},{10,11... | collective-permute-start | bytes 25165832 | tf_op jit(solution)/shard_map/ppermute | solution.py:50
  326.2 31.4 %copy-start.24 = (bf16[16,50,1024]{2,0,1:T(8,128)(2,1)S(1)}, bf16[16,50,1024]{2,0,1:T(8,128)(2,1)}, u32[]{:S(2)}) copy-start(bf16[16,50,1024]{2,0,1:T(8,128)(2,1)} %param.31) | copy-start | bytes 4915204
  390.7 9.3 %copy-start.7 = (f32[4,2,2,2,128,1024]{5,4,3,2,1,0:T(8,128)}, f32[4,2,2,2,128,1024]{5,4,3,2,1,0:T(8,128)S(1)}, u32[]{:S(2)}) copy-start(f32[4,2,2,2,128,1024]{5,4,3,2,1,0:T(8,128)S(1)} %fusion.25) | copy-start | bytes 50331652
  390.7 9.3 %copy-start.15 = (f32[800,1024]{1,0:T(8,128)S(1)}, f32[800,1024]{1,0:T(8,128)}, u32[]{:S(2)}) copy-start(f32[800,1024]{1,0:T(8,128)} %copy-done.13) | copy-start | bytes 9830404
  390.7 9.3 %copy-start.64 = (f32[1024]{0:T(1024)S(1)}, f32[1024]{0:T(1024)}, u32[]{:S(2)}) copy-start(f32[1024]{0:T(1024)} %param.30) | copy-start | bytes 12292
  400.0 167.0 %collective-permute-start.24 = (f32[4,2,2,128,1024]{4,3,2,1,0:T(8,128)}, f32[4,2,2,128,1024]{4,3,2,1,0:T(8,128)}, u32[]{:S(2)}, u32[]{:S(2)}) collective-permute-start(f32[4,2,2,128,1024]{4,3,2,1,0:T(8,128)} %dynamic-slice_bitcast_fusion), channel_id=1, source_target_pairs={{0,1},{1,0},{2,3},{3,2},{4,5},{5,4},{6,7},{7,6},{8,9},{9,8},{10,11... | collective-permute-start | bytes 25165832 | tf_op jit(solution)/shard_map/ppermute | solution.py:50
  415.7 9.6 %copy-start.18 = (f32[800,1024]{1,0:T(8,128)S(1)}, f32[800,1024]{1,0:T(8,128)}, u32[]{:S(2)}) copy-start(f32[800,1024]{1,0:T(8,128)} %copy-done.17) | copy-start | bytes 9830404
  419.9 15.2 %collective-permute-start.9 = (f32[4,2,32,512]{3,2,1,0:T(8,128)S(1)}, f32[4,2,32,512]{3,2,1,0:T(8,128)}, u32[]{:S(2)}, u32[]{:S(2)}) collective-permute-start(f32[4,2,32,512]{3,2,1,0:T(8,128)S(1)} %dynamic-slice_bitcast_fusion.15), channel_id=1, source_target_pairs={{0,4},{4,0},{8,12},{12,8},{16,20},{20,16},{24,28},{28,24},{1,5},{5... | collective-permute-start | bytes 1572872 | tf_op jit(solution)/shard_map/ppermute | solution.py:50
  423.8 14.4 %collective-permute-start.11 = (f32[4,2,32,512]{3,2,1,0:T(8,128)}, f32[4,2,32,512]{3,2,1,0:T(8,128)S(1)}, u32[]{:S(2)}, u32[]{:S(2)}) collective-permute-start(f32[4,2,32,512]{3,2,1,0:T(8,128)} %dynamic-slice_bitcast_fusion.14), channel_id=1, source_target_pairs={{0,2},{1,3},{2,0},{3,1},{4,6},{5,7},{6,4},{7,5},{8,10},{9,11},{10,... | collective-permute-start | bytes 1572872 | tf_op jit(solution)/shard_map/ppermute | solution.py:50
  427.4 7.7 %copy-start.29 = (f32[4,2,2,32,512]{4,3,2,1,0:T(8,128)S(1)}, f32[4,2,2,32,512]{4,3,2,1,0:T(8,128)}, u32[]{:S(2)}) copy-start(f32[4,2,2,32,512]{4,3,2,1,0:T(8,128)} %copy-done.28) | copy-start | bytes 3145732
  436.3 7.8 %collective-permute-start.10 = (f32[4,32,512]{2,1,0:T(8,128)S(1)}, f32[4,32,512]{2,1,0:T(8,128)S(1)}, u32[]{:S(2)}, u32[]{:S(2)}) collective-permute-start(f32[4,32,512]{2,1,0:T(8,128)S(1)} %dynamic-slice_bitcast_fusion.17), channel_id=1, source_target_pairs={{0,2},{1,3},{2,0},{3,1},{4,6},{5,7},{6,4},{7,5},{8,10},{9,11},{10,... | collective-permute-start | bytes 786440 | tf_op jit(solution)/shard_map/ppermute | solution.py:50
  438.3 15.0 %collective-permute-start.12 = (f32[4,32,512]{2,1,0:T(8,128)S(1)}, f32[4,32,512]{2,1,0:T(8,128)S(1)}, u32[]{:S(2)}, u32[]{:S(2)}) collective-permute-start(f32[4,32,512]{2,1,0:T(8,128)S(1)} %dynamic-slice_bitcast_fusion.16), channel_id=1, source_target_pairs={{0,4},{4,0},{8,12},{12,8},{16,20},{20,16},{24,28},{28,24},{1,5},{5... | collective-permute-start | bytes 786440 | tf_op jit(solution)/shard_map/ppermute | solution.py:50
  450.5 12.8 %copy-start.20 = (f32[4,2,2,32,1536]{4,3,2,1,0:T(8,128)}, f32[4,2,2,32,1536]{4,3,2,1,0:T(8,128)S(1)}, u32[]{:S(2)}) copy-start(f32[4,2,2,32,1536]{4,3,2,1,0:T(8,128)S(1)} %get-tuple-element.100) | copy-start | bytes 9437188
  450.5 12.8 %copy-start.21 = (f32[4,2,2,32,1536]{4,3,2,1,0:T(8,128)}, f32[4,2,2,32,1536]{4,3,2,1,0:T(8,128)S(1)}, u32[]{:S(2)}) copy-start(f32[4,2,2,32,1536]{4,3,2,1,0:T(8,128)S(1)} %get-tuple-element.101) | copy-start | bytes 9437188
  450.5 9.4 %copy-start.11 = (f32[16,50,1024]{2,1,0:T(8,128)S(1)}, f32[16,50,1024]{2,1,0:T(8,128)}, u32[]{:S(2)}) copy-start(f32[16,50,1024]{2,1,0:T(8,128)} %reshape.355) | copy-start | bytes 9830404
  450.5 9.4 %copy-start.35 = (s32[16,50]{1,0:T(8,128)S(1)}, s32[16,50]{1,0:T(8,128)}, u32[]{:S(2)}) copy-start(s32[16,50]{1,0:T(8,128)} %copy-done.34) | copy-start | bytes 9604
  450.5 9.4 %copy-start.44 = (pred[16,50]{1,0:T(8,128)(4,1)S(1)}, pred[16,50]{1,0:T(8,128)(4,1)}, u32[]{:S(2)}) copy-start(pred[16,50]{1,0:T(8,128)(4,1)} %copy-done.43) | copy-start | bytes 2404
  451.8 85.0 %collective-permute-start.1 = (f32[4,2,32,1536]{3,2,1,0:T(8,128)}, f32[4,2,32,1536]{3,2,1,0:T(8,128)}, u32[]{:S(2)}, u32[]{:S(2)}) collective-permute-start(f32[4,2,32,1536]{3,2,1,0:T(8,128)} %dynamic-slice_bitcast_fusion.7), channel_id=1, source_target_pairs={{0,4},{4,0},{8,12},{12,8},{16,20},{20,16},{24,28},{28,24},{1,5},{5... | collective-permute-start | bytes 4718600 | tf_op jit(solution)/shard_map/ppermute | solution.py:50
  453.3 10.1 %collective-permute-start.15 = (f32[32,1024]{1,0:T(8,128)S(1)}, f32[32,1024]{1,0:T(8,128)S(1)}, u32[]{:S(2)}, u32[]{:S(2)}) collective-permute-start(f32[32,1024]{1,0:T(8,128)S(1)} %get-tuple-element.118), channel_id=1, source_target_pairs={{0,24},{4,28},{8,0},{12,4},{16,8},{20,12},{24,16},{28,20},{1,25},{... | collective-permute-start | bytes 393224 | tf_op jit(solution)/shard_map/ppermute | solution.py:50
  458.4 83.8 %collective-permute-start.3 = (f32[4,2,32,1536]{3,2,1,0:T(8,128)}, f32[4,2,32,1536]{3,2,1,0:T(8,128)}, u32[]{:S(2)}, u32[]{:S(2)}) collective-permute-start(f32[4,2,32,1536]{3,2,1,0:T(8,128)} %dynamic-slice_bitcast_fusion.6), channel_id=1, source_target_pairs={{0,2},{1,3},{2,0},{3,1},{4,6},{5,7},{6,4},{7,5},{8,10},{9,11},{10,... | collective-permute-start | bytes 4718600 | tf_op jit(solution)/shard_map/ppermute | solution.py:50
  463.4 61.8 %collective-permute-start.14 = (f32[32,1024]{1,0:T(8,128)S(1)}, f32[32,1024]{1,0:T(8,128)S(1)}, u32[]{:S(2)}, u32[]{:S(2)}) collective-permute-start(f32[32,1024]{1,0:T(8,128)S(1)} %get-tuple-element.117), channel_id=1, source_target_pairs={{0,16},{4,20},{8,24},{12,28},{16,0},{20,4},{24,8},{28,12},{1,17},{... | collective-permute-start | bytes 393224 | tf_op jit(solution)/shard_map/ppermute | solution.py:50
  525.3 10.8 %collective-permute-start.13 = (f32[32,1024]{1,0:T(8,128)S(1)}, f32[32,1024]{1,0:T(8,128)S(1)}, u32[]{:S(2)}, u32[]{:S(2)}) collective-permute-start(f32[32,1024]{1,0:T(8,128)S(1)} %get-tuple-element.116), channel_id=1, source_target_pairs={{0,8},{4,12},{8,16},{12,20},{16,24},{20,28},{24,0},{28,4},{1,9},{5... | collective-permute-start | bytes 393224 | tf_op jit(solution)/shard_map/ppermute | solution.py:50
  538.9 19.4 %copy-start.25 = (f32[4,2,32,1536]{3,2,1,0:T(8,128)}, f32[4,2,32,1536]{3,2,1,0:T(8,128)S(1)}, u32[]{:S(2)}) copy-start(f32[4,2,32,1536]{3,2,1,0:T(8,128)S(1)} %bitcast_add_fusion.9) | copy-start | bytes 4718596
  539.9 39.1 %collective-permute-start.2 = (f32[4,32,1536]{2,1,0:T(8,128)}, f32[4,32,1536]{2,1,0:T(8,128)}, u32[]{:S(2)}, u32[]{:S(2)}) collective-permute-start(f32[4,32,1536]{2,1,0:T(8,128)} %dynamic-slice_bitcast_fusion.13), channel_id=1, source_target_pairs={{0,2},{1,3},{2,0},{3,1},{4,6},{5,7},{6,4},{7,5},{8,10},{9,11},{10,... | collective-permute-start | bytes 2359304 | tf_op jit(solution)/shard_map/ppermute | solution.py:50
  546.4 34.1 %collective-permute-start.4 = (f32[4,32,1536]{2,1,0:T(8,128)}, f32[4,32,1536]{2,1,0:T(8,128)}, u32[]{:S(2)}, u32[]{:S(2)}) collective-permute-start(f32[4,32,1536]{2,1,0:T(8,128)} %dynamic-slice_bitcast_fusion.12), channel_id=1, source_target_pairs={{0,4},{4,0},{8,12},{12,8},{16,20},{20,16},{24,28},{28,24},{1,5},{5... | collective-permute-start | bytes 2359304 | tf_op jit(solution)/shard_map/ppermute | solution.py:50
  563.8 55.4 %collective-permute-start.17 = (f32[4,2,32,2048]{3,2,1,0:T(8,128)}, f32[4,2,32,2048]{3,2,1,0:T(8,128)}, u32[]{:S(2)}, u32[]{:S(2)}) collective-permute-start(f32[4,2,32,2048]{3,2,1,0:T(8,128)} %dynamic-slice_bitcast_fusion.4), channel_id=1, source_target_pairs={{0,4},{4,0},{8,12},{12,8},{16,20},{20,16},{24,28},{28,24},{1,5},{5... | collective-permute-start | bytes 6291464 | tf_op jit(solution)/shard_map/ppermute | solution.py:50
  567.0 54.8 %collective-permute-start.19 = (f32[4,2,32,2048]{3,2,1,0:T(8,128)}, f32[4,2,32,2048]{3,2,1,0:T(8,128)}, u32[]{:S(2)}, u32[]{:S(2)}) collective-permute-start(f32[4,2,32,2048]{3,2,1,0:T(8,128)} %bitcast.291), channel_id=1, source_target_pairs={{0,2},{1,3},{2,0},{3,1},{4,6},{5,7},{6,4},{7,5},{8,10},{9,11},{10,... | collective-permute-start | bytes 6291464 | tf_op jit(solution)/shard_map/ppermute | solution.py:50
  582.1 13.4 %collective-permute-start.7 = (f32[32,3072]{1,0:T(8,128)S(1)}, f32[32,3072]{1,0:T(8,128)S(1)}, u32[]{:S(2)}, u32[]{:S(2)}) collective-permute-start(f32[32,3072]{1,0:T(8,128)S(1)} %get-tuple-element.115), channel_id=1, source_target_pairs={{0,24},{4,28},{8,0},{12,4},{16,8},{20,12},{24,16},{28,20},{1,25},{... | collective-permute-start | bytes 1179656 | tf_op jit(solution)/shard_map/ppermute | solution.py:50
  585.9 31.0 %collective-permute-start.6 = (f32[32,3072]{1,0:T(8,128)S(1)}, f32[32,3072]{1,0:T(8,128)S(1)}, u32[]{:S(2)}, u32[]{:S(2)}) collective-permute-start(f32[32,3072]{1,0:T(8,128)S(1)} %get-tuple-element.114), channel_id=1, source_target_pairs={{0,16},{4,20},{8,24},{12,28},{16,0},{20,4},{24,8},{28,12},{1,17},{... | collective-permute-start | bytes 1179656 | tf_op jit(solution)/shard_map/ppermute | solution.py:50
  585.9 32.4 %collective-permute-start.5 = (f32[32,3072]{1,0:T(8,128)S(1)}, f32[32,3072]{1,0:T(8,128)S(1)}, u32[]{:S(2)}, u32[]{:S(2)}) collective-permute-start(f32[32,3072]{1,0:T(8,128)S(1)} %get-tuple-element.113), channel_id=1, source_target_pairs={{0,8},{4,12},{8,16},{12,20},{16,24},{20,28},{24,0},{28,4},{1,9},{5... | collective-permute-start | bytes 1179656 | tf_op jit(solution)/shard_map/ppermute | solution.py:50
  595.5 62.0 %collective-permute-start.25 = (f32[4,2,128,512]{3,2,1,0:T(8,128)S(1)}, f32[4,2,128,512]{3,2,1,0:T(8,128)S(1)}, u32[]{:S(2)}, u32[]{:S(2)}) collective-permute-start(f32[4,2,128,512]{3,2,1,0:T(8,128)S(1)} %dynamic-slice_bitcast_fusion.3), channel_id=1, source_target_pairs={{0,4},{4,0},{8,12},{12,8},{16,20},{20,16},{24,28},{28,24},{1,5},{5... | collective-permute-start | bytes 6291464 | tf_op jit(solution)/shard_map/ppermute | solution.py:50
  616.9 48.6 %collective-permute-start.27 = (f32[4,2,128,512]{3,2,1,0:T(8,128)S(1)}, f32[4,2,128,512]{3,2,1,0:T(8,128)S(1)}, u32[]{:S(2)}, u32[]{:S(2)}) collective-permute-start(f32[4,2,128,512]{3,2,1,0:T(8,128)S(1)} %dynamic-slice_bitcast_fusion.2), channel_id=1, source_target_pairs={{0,2},{1,3},{2,0},{3,1},{4,6},{5,7},{6,4},{7,5},{8,10},{9,11},{10,... | collective-permute-start | bytes 6291464 | tf_op jit(solution)/shard_map/ppermute | solution.py:50
  621.2 66.8 %collective-permute-start.18 = (f32[4,32,2048]{2,1,0:T(8,128)S(1)}, f32[4,32,2048]{2,1,0:T(8,128)S(1)}, u32[]{:S(2)}, u32[]{:S(2)}) collective-permute-start(f32[4,32,2048]{2,1,0:T(8,128)S(1)} %dynamic-slice_bitcast_fusion.11), channel_id=1, source_target_pairs={{0,2},{1,3},{2,0},{3,1},{4,6},{5,7},{6,4},{7,5},{8,10},{9,11},{10,... | collective-permute-start | bytes 3145736 | tf_op jit(solution)/shard_map/ppermute | solution.py:50
  623.8 64.3 %collective-permute-start.20 = (f32[4,32,2048]{2,1,0:T(8,128)S(1)}, f32[4,32,2048]{2,1,0:T(8,128)S(1)}, u32[]{:S(2)}, u32[]{:S(2)}) collective-permute-start(f32[4,32,2048]{2,1,0:T(8,128)S(1)} %dynamic-slice_bitcast_fusion.10), channel_id=1, source_target_pairs={{0,4},{4,0},{8,12},{12,8},{16,20},{20,16},{24,28},{28,24},{1,5},{5... | collective-permute-start | bytes 3145736 | tf_op jit(solution)/shard_map/ppermute | solution.py:50
  658.1 48.1 %collective-permute-start.26 = (f32[4,128,512]{2,1,0:T(8,128)S(1)}, f32[4,128,512]{2,1,0:T(8,128)S(1)}, u32[]{:S(2)}, u32[]{:S(2)}) collective-permute-start(f32[4,128,512]{2,1,0:T(8,128)S(1)} %dynamic-slice_bitcast_fusion.9), channel_id=1, source_target_pairs={{0,2},{1,3},{2,0},{3,1},{4,6},{5,7},{6,4},{7,5},{8,10},{9,11},{10,... | collective-permute-start | bytes 3145736 | tf_op jit(solution)/shard_map/ppermute | solution.py:50
  666.0 40.3 %collective-permute-start.28 = (f32[4,128,512]{2,1,0:T(8,128)S(1)}, f32[4,128,512]{2,1,0:T(8,128)S(1)}, u32[]{:S(2)}, u32[]{:S(2)}) collective-permute-start(f32[4,128,512]{2,1,0:T(8,128)S(1)} %dynamic-slice_bitcast_fusion.8), channel_id=1, source_target_pairs={{0,4},{4,0},{8,12},{12,8},{16,20},{20,16},{24,28},{28,24},{1,5},{5... | collective-permute-start | bytes 3145736 | tf_op jit(solution)/shard_map/ppermute | solution.py:50
  688.4 18.5 %collective-permute-start.23 = (f32[32,4096]{1,0:T(8,128)S(1)}, f32[32,4096]{1,0:T(8,128)S(1)}, u32[]{:S(2)}, u32[]{:S(2)}) collective-permute-start(f32[32,4096]{1,0:T(8,128)S(1)} %get-tuple-element.110), channel_id=1, source_target_pairs={{0,24},{4,28},{8,0},{12,4},{16,8},{20,12},{24,16},{28,20},{1,25},{... | collective-permute-start | bytes 1572872 | tf_op jit(solution)/shard_map/ppermute | solution.py:50
  688.4 67.9 %collective-permute-start.22 = (f32[32,4096]{1,0:T(8,128)S(1)}, f32[32,4096]{1,0:T(8,128)S(1)}, u32[]{:S(2)}, u32[]{:S(2)}) collective-permute-start(f32[32,4096]{1,0:T(8,128)S(1)} %get-tuple-element.109), channel_id=1, source_target_pairs={{0,16},{4,20},{8,24},{12,28},{16,0},{20,4},{24,8},{28,12},{1,17},{... | collective-permute-start | bytes 1572872 | tf_op jit(solution)/shard_map/ppermute | solution.py:50
  688.5 67.8 %collective-permute-start.21 = (f32[32,4096]{1,0:T(8,128)S(1)}, f32[32,4096]{1,0:T(8,128)S(1)}, u32[]{:S(2)}, u32[]{:S(2)}) collective-permute-start(f32[32,4096]{1,0:T(8,128)S(1)} %get-tuple-element.108), channel_id=1, source_target_pairs={{0,8},{4,12},{8,16},{12,20},{16,24},{20,28},{24,0},{28,4},{1,9},{5... | collective-permute-start | bytes 1572872 | tf_op jit(solution)/shard_map/ppermute | solution.py:50
  706.7 50.5 %collective-permute-start.31 = (f32[128,1024]{1,0:T(8,128)S(1)}, f32[128,1024]{1,0:T(8,128)S(1)}, u32[]{:S(2)}, u32[]{:S(2)}) collective-permute-start(f32[128,1024]{1,0:T(8,128)S(1)} %get-tuple-element.107), channel_id=1, source_target_pairs={{0,24},{4,28},{8,0},{12,4},{16,8},{20,12},{24,16},{28,20},{1,25},{... | collective-permute-start | bytes 1572872 | tf_op jit(solution)/shard_map/ppermute | solution.py:50
  706.8 63.5 %collective-permute-start.30 = (f32[128,1024]{1,0:T(8,128)S(1)}, f32[128,1024]{1,0:T(8,128)S(1)}, u32[]{:S(2)}, u32[]{:S(2)}) collective-permute-start(f32[128,1024]{1,0:T(8,128)S(1)} %get-tuple-element.106), channel_id=1, source_target_pairs={{0,16},{4,20},{8,24},{12,28},{16,0},{20,4},{24,8},{28,12},{1,17},{... | collective-permute-start | bytes 1572872 | tf_op jit(solution)/shard_map/ppermute | solution.py:50
  706.9 64.4 %copy-start.1 = (bf16[1024,1024]{1,0:T(8,128)(2,1)S(1)}, bf16[1024,1024]{1,0:T(8,128)(2,1)}, u32[]{:S(2)}) copy-start(bf16[1024,1024]{1,0:T(8,128)(2,1)} %param.23) | copy-start | bytes 6291460
  706.9 63.4 %collective-permute-start.29 = (f32[128,1024]{1,0:T(8,128)S(1)}, f32[128,1024]{1,0:T(8,128)S(1)}, u32[]{:S(2)}, u32[]{:S(2)}) collective-permute-start(f32[128,1024]{1,0:T(8,128)S(1)} %get-tuple-element.105), channel_id=1, source_target_pairs={{0,8},{4,12},{8,16},{12,20},{16,24},{20,28},{24,0},{28,4},{1,9},{5... | collective-permute-start | bytes 1572872 | tf_op jit(solution)/shard_map/ppermute | solution.py:50
  (33 other events, 139.8 us)
